TPU v7x, 32 devices: a whole 2x2x4 slice. The times are simulated.
32 devices in a mesh: member: 2 (over y), tile: 4 (over z), face: 4 (over x, core).
Axes of the slice: x: 2, y: 2, z: 4, core: 2. Of those that a mesh axis runs over, the one named last changes fastest.
Arguments:
- atmosphere: float32 [6, 4, 16, 32, 32], P('member', 'face', None, 'tile'), parts along dimension 0, may hold values from -6 to 6
- weight_in: bfloat16 [3, 3, 90, 16], replicated, may hold values from -0.5 to 0.5
- weight_block: bfloat16 [3, 3, 90, 90], replicated, may hold values from -0.21875 to 0.21875
- weight_mix: bfloat16 [90, 90], replicated, may hold values from -0.625 to 0.625
- weight_down: bfloat16 [3, 3, 180, 90], replicated, may hold values from -0.21875 to 0.21875
- weight_coarse: bfloat16 [3, 3, 180, 180], replicated, may hold values from -0.15625 to 0.15625
- weight_decode: bfloat16 [3, 3, 90, 270], replicated, may hold values from -0.125 to 0.125
- readout_matrix: bfloat16 [16, 90], replicated, may hold values from -0.625 to 0.625
Outputs:
- advanced_state: float32 [6, 4, 16, 32, 32], P('member', 'face', None, 'tile'), parts along dimension 0
There are 2 independent parts, one for each index of `member`. A program takes and returns all parts, laid end to end along the dimension named above; an argument that names none is the same for every part. Nothing has to cross between parts.
All inputs are finite; a program needn't handle non-finite values.
Results may differ from a plain program's by a relative error of at most 0.0021.
Values may be sent and summed in bfloat16 or wider, within the bound.
A program may use at most 128 MiB of HBM per device.

v0:
```python
import jax
import jax.numpy as jnp
from jax import lax
from jax.sharding import PartitionSpec as P


def passed_along(block, axis, distance):
    devices = range(lax.axis_size(axis))
    route = [((i - distance) % len(devices), i) for i in devices]
    return lax.ppermute(block, axis, route)


def padded_2(array, sides, width):
    for axis, dim in sides:
        size, length = (lax.axis_size(axis), array.shape[dim])
        up = [(i, (i + 1) % size) for i in range(size)]
        down = [(j, i) for i, j in up]
        last = lax.slice_in_dim(array, length - width, length, axis=dim)
        initial = lax.slice_in_dim(array, 0, width, axis=dim)
        before = lax.ppermute(last, axis, up)
        after = lax.ppermute(initial, axis, down)
        array = jnp.concatenate([before, array, after], axis=dim)
    return array


def zero_corners(rim_rows, halo_width):
    corner = jnp.zeros(rim_rows.shape[:-1] + (halo_width,), rim_rows.dtype)
    return jnp.concatenate([corner, rim_rows[..., halo_width:-halo_width], corner], -1)


def turned_rows(column_block, halo_width):
    corner = jnp.zeros(column_block.shape[:-2] + (halo_width, halo_width), column_block.dtype)
    turned_strip = jnp.flip(jnp.swapaxes(column_block, -1, -2), -2)
    return jnp.concatenate([corner, turned_strip, corner], -1)


def pad_strip(strip_data, halo_width):
    row_count = strip_data.shape[2]
    col_count = strip_data.shape[3]
    tile_count = lax.axis_size("tile")
    tile_pos = lax.axis_index("tile")
    rim_start = col_count - halo_width
    polar_rows = jnp.stack(
        [strip_data[0, :, :halo_width, :], strip_data[2, :, row_count - halo_width :, :]]
    )
    west_cols = jnp.stack([strip_data[0, :, :, rim_start:], strip_data[1, :, :, rim_start:]])
    polar_prev, preceding_sunset_neighbour = passed_along((polar_rows, west_cols), "face", 1)
    east_cols = jnp.stack(
        [
            strip_data[1, :, :, :halo_width],
            strip_data[2, :, :, :halo_width],
            strip_data[0, :, :, :halo_width],
            strip_data[2, :, :, rim_start:],
        ]
    )
    following_sunrise_neighbour = passed_along(east_cols, "face", -1)
    polar_cols = lax.all_gather(following_sunrise_neighbour[2:], "tile", axis=2, tiled=True)
    owner_mask = jnp.stack([tile_pos == 0, tile_pos == tile_count - 1]).reshape(2, 1, 1, 1)
    masked_rows = jnp.where(owner_mask, polar_prev, jnp.zeros_like(polar_prev)).astype(jnp.float32)
    pieces = lax.psum_scatter(
        masked_rows.astype(jnp.bfloat16), "tile", scatter_dimension=3, tiled=True
    )
    left_cols = jnp.stack(
        [
            jnp.flip(jnp.swapaxes(pieces[0], -1, -2), -1),
            preceding_sunset_neighbour[0],
            preceding_sunset_neighbour[1],
        ]
    )
    right_cols = jnp.stack(
        [
            following_sunrise_neighbour[0],
            following_sunrise_neighbour[1],
            jnp.flip(jnp.swapaxes(pieces[1], -1, -2), -1),
        ]
    )
    extended = jnp.concatenate([left_cols, strip_data, right_cols], -1)
    padded = padded_2(extended, (("tile", 2),), halo_width)
    upper_got = padded[:, :, :halo_width, :]
    lower_got = padded[:, :, padded.shape[2] - halo_width :, :]
    upper_face = jnp.stack(
        [
            turned_rows(polar_cols[0], halo_width),
            zero_corners(upper_got[0], halo_width),
            zero_corners(upper_got[1], halo_width),
        ]
    )
    lower_face = jnp.stack(
        [
            zero_corners(lower_got[1], halo_width),
            zero_corners(lower_got[2], halo_width),
            turned_rows(polar_cols[1], halo_width),
        ]
    )
    upper_rows = jnp.where(tile_pos == 0, upper_face, upper_got)
    lower_rows = jnp.where(tile_pos == tile_count - 1, lower_face, lower_got)
    return jnp.concatenate(
        [upper_rows, padded[:, :, halo_width : padded.shape[2] - halo_width, :], lower_rows], 2
    )


def convolve(padded, weight, dilation):
    row_count = padded.shape[2] - 2 * dilation
    col_count = padded.shape[3] - 2 * dilation
    summed = None
    for row_tap in range(3):
        for col_tap in range(3):
            window_patch = padded[
                :,
                :,
                row_tap * dilation : row_tap * dilation + row_count,
                col_tap * dilation : col_tap * dilation + col_count,
            ]
            product = jnp.einsum(
                "oc,fcrn->forn",
                weight[row_tap, col_tap],
                window_patch,
                preferred_element_type=jnp.float32,
            )
            summed = product if summed is None else summed + product
    return summed


def pool_cells(values):
    shape = values.shape
    wide = values.astype(jnp.float32).reshape(shape[:-2] + (shape[-2] // 2, 2, shape[-1] // 2, 2))
    return jnp.mean(wide, axis=(-3, -1))


def upsample(values):
    shape = values.shape
    grown = jnp.broadcast_to(
        values[..., :, None, :, None], shape[:-2] + (shape[-2], 2, shape[-1], 2)
    )
    return grown.reshape(shape[:-2] + (2 * shape[-2], 2 * shape[-1]))


def per_cell_channel_blend(weight, values):
    return jnp.einsum("oc,fcrn->forn", weight, values, preferred_element_type=jnp.float32)


def shards(
    atmosphere,
    weight_in,
    weight_block,
    weight_mix,
    weight_down,
    weight_coarse,
    weight_decode,
    readout_matrix,
):
    variable_grids = atmosphere[:, 0]
    source = variable_grids.astype(jnp.bfloat16)
    encoded = jax.nn.gelu(convolve(pad_strip(source, 1), weight_in, 1)).astype(jnp.bfloat16)
    inner_out = jax.nn.gelu(convolve(pad_strip(encoded, 1), weight_block, 1)).astype(jnp.bfloat16)
    skip_level = (
        encoded.astype(jnp.float32) + per_cell_channel_blend(weight_mix, inner_out)
    ).astype(jnp.bfloat16)
    pooled = pool_cells(skip_level).astype(jnp.bfloat16)
    coarse_one = jax.nn.gelu(convolve(pad_strip(pooled, 2), weight_down, 2)).astype(jnp.bfloat16)
    coarse_two = (
        coarse_one.astype(jnp.float32)
        + jax.nn.gelu(convolve(pad_strip(coarse_one, 1), weight_coarse, 1))
    ).astype(jnp.bfloat16)
    joined_features = jnp.concatenate([upsample(coarse_two), skip_level], 1)
    padded = pad_strip(joined_features, 1)
    upscaled_activations = jax.nn.gelu(convolve(padded, weight_decode, 1)).astype(jnp.bfloat16)
    advanced_state = variable_grids + per_cell_channel_blend(readout_matrix, upscaled_activations)
    return advanced_state[:, None]


def solution(mesh):
    in_specs = (P("member", "face", None, "tile", None), P(), P(), P(), P(), P(), P(), P())
    out_specs = P("member", "face", None, "tile", None)
    return jax.shard_map(shards, mesh=mesh, in_specs=in_specs, out_specs=out_specs, check_vma=False)
```

profile of v0, /device:TPU:0, one launch (start us, length us, event | category | flops | bytes accessed | tf_op | source)
XLA Modules:
  0.0 224.8 jit_solution(17048535610313699755)
XLA Ops:
  6.5 1.0 copy.325
  7.7 0.5 collective-permute-start.1
  8.3 2.7 %collective-permute-start.2 = (bf16[2,16,8,1]{3,1,2,0:T(8,128)(2,1)S(1)}, bf16[2,16,8,1]{3,1,2,0:T(8,128)(2,1)S(1)}, u32[]{:S(2)}, u32[]{:S(2)}) collective-permute-start(bf16[2,16,8,1]{3,1,2,0:T(8,128)(2,1)S(1)} %get-tuple-element.44), channel_id=1, source_target_pairs={{3,0},{0,1},{1,2},{2,3},{7,4},{4,5},{5,6},{6,7},{11,8},{8,9},{9,10... | collective-permute-start | bytes 1544 | tf_op jit(solution)/shard_map/ppermute | solution.py:10
  11.5 0.6 dynamic-slice
  13.8 13.5 %all_gather.15 = bf16[2,16,32,1]{1,0,3,2:T(2,128)(2,1)S(1)} all-gather(bf16[2,16,8,1]{1,0,3,2:T(2,128)(2,1)S(1)} %copy.152), channel_id=1, replica_groups=mesh['member'=2,'tile'=4,'face'=4] {'tile'}, dimensions={2}, use_global_device_ids=true | all-gather | bytes 2560 | tf_op jit(solution)/shard_map/all_gather | solution.py:57
  27.4 18.8 %all-reduce = bf16[2,16,1,32]{1,0,2,3:T(2,128)(2,1)S(1)} all-reduce(bf16[2,16,1,32]{1,0,2,3:T(2,128)(2,1)S(1)} %broadcast_select_fusion.1), channel_id=2, replica_groups=mesh['member'=2,'tile'=4,'face'=4] {'tile'}, use_global_device_ids=true, to_apply=%region_0.1.clone | all-reduce | flops 1024 | bytes 4096
  46.9 2.0 collective-permute-start.3
  48.9 1.5 collective-permute-done.4
  50.5 1.9 collective-permute-done.3
  55.2 0.4 fusion.31
  55.7 1.7 collective-permute-start.6
  57.8 1.1 collective-permute-done.6
  59.1 0.7 reshape.86
  59.9 13.1 %all_gather.16 = bf16[2,90,32,1]{1,3,2,0:T(2,128)(2,1)S(1)} all-gather(bf16[2,90,8,1]{1,3,2,0:T(2,128)(2,1)S(1)} %get-tuple-element.94), channel_id=1, replica_groups=mesh['member'=2,'tile'=4,'face'=4] {'tile'}, dimensions={2}, use_global_device_ids=true | all-gather | bytes 14400 | tf_op jit(solution)/shard_map/all_gather | solution.py:57
  73.0 4.1 %reduce-scatter.7.cloned.1.call-done = bf16[8,180]{1,0:T(8,128)(2,1)} async-done(((bf16[32,180]{1,0:T(8,128)(2,1)}), bf16[8,180]{1,0:T(8,128)(2,1)}) %reduce-scatter.7.cloned.1.call-update) | async-done | bytes 2896
  77.2 0.7 reshape.87
  78.1 0.6 collective-permute-start.9
  78.7 1.6 collective-permute-start.8
  80.2 1.8 collective-permute-done.9
  82.0 2.4 %collective-permute-done.8 = bf16[3,90,1,34]{1,3,2,0:T(8,128)(2,1)S(1)} collective-permute-done((bf16[3,90,1,34]{1,3,2,0:T(8,128)(2,1)S(1)}, bf16[3,90,1,34]{1,3,2,0:T(8,128)(2,1)S(1)}, u32[]{:S(2)}, u32[]{:S(2)}) %collective-permute-start.8) | collective-permute-done | bytes 18392 | tf_op jit(solution)/shard_map/ppermute | solution.py:20
  87.3 1.8 collective-permute-start.10
  89.3 1.1 collective-permute-done.10
  90.5 13.1 %all_gather.17 = bf16[2,90,16,2]{1,3,0,2:T(2,128)(2,1)S(1)} all-gather(bf16[2,90,4,2]{1,3,0,2:T(2,128)(2,1)S(1)} %copy.163), channel_id=1, replica_groups=mesh['member'=2,'tile'=4,'face'=4] {'tile'}, dimensions={2}, use_global_device_ids=true | all-gather | bytes 14400 | tf_op jit(solution)/shard_map/all_gather | solution.py:57
  103.7 15.5 %all-reduce.1 = bf16[2,90,2,16]{1,3,2,0:T(8,128)(2,1)S(1)} all-reduce(bf16[2,90,2,16]{1,3,2,0:T(8,128)(2,1)S(1)} %broadcast_select_fusion.3), channel_id=4, replica_groups=mesh['member'=2,'tile'=4,'face'=4] {'tile'}, use_global_device_ids=true, to_apply=%region_3.4.clone | all-reduce | flops 5760 | bytes 23040
  119.3 1.0 collective-permute-start.14
  120.4 1.2 collective-permute-start.13
  121.5 1.8 collective-permute-done.14
  123.4 2.8 %collective-permute-done.13 = bf16[3,90,2,20]{1,3,2,0:T(8,128)(2,1)S(1)} collective-permute-done((bf16[3,90,2,20]{1,3,2,0:T(8,128)(2,1)S(1)}, bf16[3,90,2,20]{1,3,2,0:T(8,128)(2,1)S(1)}, u32[]{:S(2)}, u32[]{:S(2)}) %collective-permute-start.13) | collective-permute-done | bytes 21632 | tf_op jit(solution)/shard_map/ppermute | solution.py:20
  128.2 1.6 collective-permute-start.16
  130.3 1.2 collective-permute-done.15
  131.6 13.1 %all_gather.18 = bf16[2,180,16,1]{1,3,2,0:T(2,128)(2,1)S(1)} all-gather(bf16[2,180,4,1]{1,3,2,0:T(2,128)(2,1)S(1)} %get-tuple-element.86), channel_id=1, replica_groups=mesh['member'=2,'tile'=4,'face'=4] {'tile'}, dimensions={2}, use_global_device_ids=true | all-gather | bytes 14400 | tf_op jit(solution)/shard_map/all_gather | solution.py:57
  144.8 15.5 %all-reduce.2 = bf16[2,180,1,16]{1,3,2,0:T(8,128)(2,1)S(1)} all-reduce(bf16[2,180,1,16]{1,3,2,0:T(8,128)(2,1)S(1)} %broadcast_select_fusion.2), channel_id=5, replica_groups=mesh['member'=2,'tile'=4,'face'=4] {'tile'}, use_global_device_ids=true, to_apply=%region_4.5.clone | all-reduce | flops 5760 | bytes 23040
  160.4 1.0 collective-permute-start.19
  161.4 1.2 collective-permute-start.18
  162.6 1.8 collective-permute-done.19
  164.4 2.8 %collective-permute-done.18 = bf16[3,180,1,18]{1,3,2,0:T(8,128)(2,1)S(1)} collective-permute-done((bf16[3,180,1,18]{1,3,2,0:T(8,128)(2,1)S(1)}, bf16[3,180,1,18]{1,3,2,0:T(8,128)(2,1)S(1)}, u32[]{:S(2)}, u32[]{:S(2)}) %collective-permute-start.18) | collective-permute-done | bytes 19472 | tf_op jit(solution)/shard_map/ppermute | solution.py:20
  170.3 2.0 collective-permute-start.20
  172.5 1.3 collective-permute-done.20
  173.7 13.1 %all_gather.19 = bf16[2,270,32,1]{1,2,3,0:T(8,128)(2,1)S(1)} all-gather(bf16[2,270,8,1]{1,2,3,0:T(8,128)(2,1)S(1)} %get-tuple-element.84), channel_id=1, replica_groups=mesh['member'=2,'tile'=4,'face'=4] {'tile'}, dimensions={2}, use_global_device_ids=true | all-gather | bytes 43200 | tf_op jit(solution)/shard_map/all_gather | solution.py:57
  187.1 16.2 %all-reduce.3 = bf16[2,270,1,32]{1,3,2,0:T(8,128)(2,1)S(1)} all-reduce(bf16[2,270,1,32]{1,3,2,0:T(8,128)(2,1)S(1)} %copy.172), channel_id=6, replica_groups=mesh['member'=2,'tile'=4,'face'=4] {'tile'}, use_global_device_ids=true, to_apply=%region_5.6.clone | all-reduce | flops 17280 | bytes 69120
  203.4 0.4 fusion.16
  204.0 1.9 collective-permute-start.24
  206.1 2.5 %collective-permute-done.24 = bf16[3,270,1,34]{1,3,2,0:T(8,128)(2,1)S(1)} collective-permute-done((bf16[3,270,1,34]{1,3,2,0:T(8,128)(2,1)S(1)}, bf16[3,270,1,34]{1,3,2,0:T(8,128)(2,1)S(1)}, u32[]{:S(2)}, u32[]{:S(2)}) %collective-permute-start.24) | collective-permute-done | bytes 55112 | tf_op jit(solution)/shard_map/ppermute | solution.py:21
  208.7 3.6 %collective-permute-done.23 = bf16[3,270,1,34]{1,3,2,0:T(8,128)(2,1)S(1)} collective-permute-done((bf16[3,270,1,34]{1,3,2,0:T(8,128)(2,1)S(1)}, bf16[3,270,1,34]{1,3,2,0:T(8,128)(2,1)S(1)}, u32[]{:S(2)}, u32[]{:S(2)}) %collective-permute-start.23) | collective-permute-done | bytes 55112 | tf_op jit(solution)/shard_map/ppermute | solution.py:20
  212.5 0.6 pad_maximum_fusion.1
  213.1 0.5 copy-done.4
  216.6 0.6 fusion.10
  217.2 0.8 copy.179
  (232 shorter events, 18.2 us)
Async XLA Ops:
  6.5 79.7 %copy-start = (bf16[90,90]{1,0:T(8,128)(2,1)S(1)}, bf16[90,90]{1,0:T(8,128)(2,1)}, u32[]{:S(2)}) copy-start(bf16[90,90]{1,0:T(8,128)(2,1)} %param.11) | copy-start | bytes 48604
  6.5 4.6 %copy-start.1 = (f32[3,1,16,8,32]{4,3,2,1,0:T(8,128)S(1)}, f32[3,1,16,8,32]{4,3,2,1,0:T(8,128)}, u32[]{:S(2)}) copy-start(f32[3,1,16,8,32]{4,3,2,1,0:T(8,128)} %param.8) | copy-start | bytes 147460
  6.5 4.7 %copy-start.6 = (bf16[3,3,90,16]{2,3,1,0:T(8,128)(2,1)S(1)}, bf16[3,3,90,16]{2,3,1,0:T(8,128)(2,1)}, u32[]{:S(2)}) copy-start(bf16[3,3,90,16]{2,3,1,0:T(8,128)(2,1)} %param.9) | copy-start | bytes 77764
  6.5 70.6 %reduce-scatter.7.cloned.1.call-start = ((), (), s32[]{:S(2)}) async-start(), calls=%async_computation.1 | async-start | bytes 20480
  7.6 3.9 %copy-start.8 = (u32[32]{0:T(128)S(1)}, u32[32]{0:T(128)}, u32[]{:S(2)}) copy-start(u32[32]{0:T(128)} %constant.6) | copy-start | bytes 388
  7.7 19.6 %collective-permute-start.1 = (bf16[2,16,1,32]{1,0,2,3:T(2,128)(2,1)S(1)}, bf16[2,16,1,32]{1,0,2,3:T(2,128)(2,1)S(1)}, u32[]{:S(2)}, u32[]{:S(2)}) collective-permute-start(bf16[2,16,1,32]{1,0,2,3:T(2,128)(2,1)S(1)} %copy.154), channel_id=1, source_target_pairs={{3,0},{0,1},{1,2},{2,3},{7,4},{4,5},{5,6},{6,7},{11,8},{8,9},{9,10... | collective-permute-start | bytes 6152 | tf_op jit(solution)/shard_map/ppermute | solution.py:10
  8.3 38.2 %collective-permute-start.2 = (bf16[2,16,8,1]{3,1,2,0:T(8,128)(2,1)S(1)}, bf16[2,16,8,1]{3,1,2,0:T(8,128)(2,1)S(1)}, u32[]{:S(2)}, u32[]{:S(2)}) collective-permute-start(bf16[2,16,8,1]{3,1,2,0:T(8,128)(2,1)S(1)} %get-tuple-element.44), channel_id=1, source_target_pairs={{3,0},{0,1},{1,2},{2,3},{7,4},{4,5},{5,6},{6,7},{11,8},{8,9},{9,10... | collective-permute-start | bytes 1544 | tf_op jit(solution)/shard_map/ppermute | solution.py:10
  11.1 2.6 %collective-permute-start = (bf16[4,16,8,1]{3,1,2,0:T(8,128)(2,1)S(1)}, bf16[4,16,8,1]{3,1,2,0:T(8,128)(2,1)S(1)}, u32[]{:S(2)}, u32[]{:S(2)}) collective-permute-start(bf16[4,16,8,1]{3,1,2,0:T(8,128)(2,1)S(1)} %pad_maximum_fusion.14), channel_id=1, source_target_pairs={{1,0},{2,1},{3,2},{0,3},{5,4},{6,5},{7,6},{4,7},{9,8},{10,9},{11,1... | collective-permute-start | bytes 3080 | tf_op jit(solution)/shard_map/ppermute | solution.py:10
  46.6 3.7 %collective-permute-start.4 = (bf16[3,16,1,34]{3,1,2,0:T(8,128)(2,1)S(1)}, bf16[3,16,1,34]{3,1,2,0:T(8,128)(2,1)S(1)}, u32[]{:S(2)}, u32[]{:S(2)}) collective-permute-start(bf16[3,16,1,34]{3,1,2,0:T(8,128)(2,1)S(1)} %get-tuple-element.20), channel_id=1, source_target_pairs={{4,0},{8,4},{12,8},{0,12},{5,1},{9,5},{13,9},{1,13},{6,2},{10,6},{... | collective-permute-start | bytes 9800 | tf_op jit(solution)/shard_map/ppermute | solution.py:21
  46.9 5.5 %collective-permute-start.3 = (bf16[3,16,1,34]{3,1,2,0:T(8,128)(2,1)S(1)}, bf16[3,16,1,34]{3,1,2,0:T(8,128)(2,1)S(1)}, u32[]{:S(2)}, u32[]{:S(2)}) collective-permute-start(bf16[3,16,1,34]{3,1,2,0:T(8,128)(2,1)S(1)} %get-tuple-element.21), channel_id=1, source_target_pairs={{0,4},{4,8},{8,12},{12,0},{1,5},{5,9},{9,13},{13,1},{2,6},{6,10},{... | collective-permute-start | bytes 9800 | tf_op jit(solution)/shard_map/ppermute | solution.py:20
  55.1 2.5 %copy-start.5 = (bf16[3,3,90,90]{3,2,1,0:T(8,128)(2,1)S(1)}, bf16[3,3,90,90]{3,2,1,0:T(8,128)(2,1)}, u32[]{:S(2)}) copy-start(bf16[3,3,90,90]{3,2,1,0:T(8,128)(2,1)} %param.10) | copy-start | bytes 437404
  55.6 22.3 %collective-permute-start.7 = (bf16[2,90,8,1]{1,3,2,0:T(2,128)(2,1)S(1)}, bf16[2,90,8,1]{1,3,2,0:T(2,128)(2,1)S(1)}, u32[]{:S(2)}, u32[]{:S(2)}) collective-permute-start(bf16[2,90,8,1]{1,3,2,0:T(2,128)(2,1)S(1)} %get-tuple-element.26), channel_id=1, source_target_pairs={{3,0},{0,1},{1,2},{2,3},{7,4},{4,5},{5,6},{6,7},{11,8},{8,9},{9,10... | collective-permute-start | bytes 8648 | tf_op jit(solution)/shard_map/ppermute | solution.py:10
  55.7 3.2 %collective-permute-start.6 = (bf16[2,90,1,32]{1,3,2,0:T(8,128)(2,1)S(1)}, bf16[2,90,1,32]{1,3,2,0:T(8,128)(2,1)S(1)}, u32[]{:S(2)}, u32[]{:S(2)}) collective-permute-start(bf16[2,90,1,32]{1,3,2,0:T(8,128)(2,1)S(1)} %pad_maximum_fusion.99), channel_id=1, source_target_pairs={{3,0},{0,1},{1,2},{2,3},{7,4},{4,5},{5,6},{6,7},{11,8},{8,9},{9,10... | collective-permute-start | bytes 34568 | tf_op jit(solution)/shard_map/ppermute | solution.py:10
  57.5 2.4 %collective-permute-start.5 = (bf16[4,90,8,1]{1,3,2,0:T(2,128)(2,1)S(1)}, bf16[4,90,8,1]{1,3,2,0:T(2,128)(2,1)S(1)}, u32[]{:S(2)}, u32[]{:S(2)}) collective-permute-start(bf16[4,90,8,1]{1,3,2,0:T(2,128)(2,1)S(1)} %pad_maximum_fusion.98), channel_id=1, source_target_pairs={{1,0},{2,1},{3,2},{0,3},{5,4},{6,5},{7,6},{4,7},{9,8},{10,9},{11,1... | collective-permute-start | bytes 17288 | tf_op jit(solution)/shard_map/ppermute | solution.py:10
  78.1 3.9 %collective-permute-start.9 = (bf16[3,90,1,34]{1,3,2,0:T(8,128)(2,1)S(1)}, bf16[3,90,1,34]{1,3,2,0:T(8,128)(2,1)S(1)}, u32[]{:S(2)}, u32[]{:S(2)}) collective-permute-start(bf16[3,90,1,34]{1,3,2,0:T(8,128)(2,1)S(1)} %get-tuple-element.24), channel_id=1, source_target_pairs={{4,0},{8,4},{12,8},{0,12},{5,1},{9,5},{13,9},{1,13},{6,2},{10,6},{... | collective-permute-start | bytes 55088 | tf_op jit(solution)/shard_map/ppermute | solution.py:21
  78.7 5.7 %collective-permute-start.8 = (bf16[3,90,1,34]{1,3,2,0:T(8,128)(2,1)S(1)}, bf16[3,90,1,34]{1,3,2,0:T(8,128)(2,1)S(1)}, u32[]{:S(2)}, u32[]{:S(2)}) collective-permute-start(bf16[3,90,1,34]{1,3,2,0:T(8,128)(2,1)S(1)} %get-tuple-element.25), channel_id=1, source_target_pairs={{0,4},{4,8},{8,12},{12,0},{1,5},{5,9},{9,13},{13,1},{2,6},{6,10},{... | collective-permute-start | bytes 55088 | tf_op jit(solution)/shard_map/ppermute | solution.py:20
  86.7 2.4 %copy-start.3 = (bf16[3,3,180,90]{3,2,1,0:T(8,128)(2,1)S(1)}, bf16[3,3,180,90]{3,2,1,0:T(8,128)(2,1)}, u32[]{:S(2)}) copy-start(bf16[3,3,180,90]{3,2,1,0:T(8,128)(2,1)} %param.12) | copy-start | bytes 874804
  87.2 32.1 %collective-permute-start.12 = (bf16[2,90,4,2]{1,3,2,0:T(2,128)(2,1)S(1)}, bf16[2,90,4,2]{1,3,2,0:T(2,128)(2,1)S(1)}, u32[]{:S(2)}, u32[]{:S(2)}) collective-permute-start(bf16[2,90,4,2]{1,3,2,0:T(2,128)(2,1)S(1)} %get-tuple-element.62), channel_id=1, source_target_pairs={{3,0},{0,1},{1,2},{2,3},{7,4},{4,5},{5,6},{6,7},{11,8},{8,9},{9,10... | collective-permute-start | bytes 8648 | tf_op jit(solution)/shard_map/ppermute | solution.py:10
  87.3 3.1 %collective-permute-start.10 = (bf16[4,90,4,2]{1,3,2,0:T(2,128)(2,1)S(1)}, bf16[4,90,4,2]{1,3,2,0:T(2,128)(2,1)S(1)}, u32[]{:S(2)}, u32[]{:S(2)}) collective-permute-start(bf16[4,90,4,2]{1,3,2,0:T(2,128)(2,1)S(1)} %pad_maximum_fusion.119), channel_id=1, source_target_pairs={{1,0},{2,1},{3,2},{0,3},{5,4},{6,5},{7,6},{4,7},{9,8},{10,9},{11,1... | collective-permute-start | bytes 17288 | tf_op jit(solution)/shard_map/ppermute | solution.py:10
  89.3 14.3 %collective-permute-start.11 = (bf16[2,90,2,16]{1,3,2,0:T(8,128)(2,1)S(1)}, bf16[2,90,2,16]{1,3,2,0:T(8,128)(2,1)S(1)}, u32[]{:S(2)}, u32[]{:S(2)}) collective-permute-start(bf16[2,90,2,16]{1,3,2,0:T(8,128)(2,1)S(1)} %pad_maximum_fusion.100), channel_id=1, source_target_pairs={{3,0},{0,1},{1,2},{2,3},{7,4},{4,5},{5,6},{6,7},{11,8},{8,9},{9,10... | collective-permute-start | bytes 34568 | tf_op jit(solution)/shard_map/ppermute | solution.py:10
  119.3 4.0 %collective-permute-start.14 = (bf16[3,90,2,20]{1,3,2,0:T(8,128)(2,1)S(1)}, bf16[3,90,2,20]{1,3,2,0:T(8,128)(2,1)S(1)}, u32[]{:S(2)}, u32[]{:S(2)}) collective-permute-start(bf16[3,90,2,20]{1,3,2,0:T(8,128)(2,1)S(1)} %get-tuple-element.54), channel_id=1, source_target_pairs={{4,0},{8,4},{12,8},{0,12},{5,1},{9,5},{13,9},{1,13},{6,2},{10,6},{... | collective-permute-start | bytes 64808 | tf_op jit(solution)/shard_map/ppermute | solution.py:21
  120.4 5.8 %collective-permute-start.13 = (bf16[3,90,2,20]{1,3,2,0:T(8,128)(2,1)S(1)}, bf16[3,90,2,20]{1,3,2,0:T(8,128)(2,1)S(1)}, u32[]{:S(2)}, u32[]{:S(2)}) collective-permute-start(bf16[3,90,2,20]{1,3,2,0:T(8,128)(2,1)S(1)} %get-tuple-element.55), channel_id=1, source_target_pairs={{0,4},{4,8},{8,12},{12,0},{1,5},{5,9},{9,13},{13,1},{2,6},{6,10},{... | collective-permute-start | bytes 64808 | tf_op jit(solution)/shard_map/ppermute | solution.py:20
  127.4 2.7 %copy-start.2 = (bf16[3,3,180,180]{3,2,1,0:T(8,128)(2,1)S(1)}, bf16[3,3,180,180]{3,2,1,0:T(8,128)(2,1)}, u32[]{:S(2)}) copy-start(bf16[3,3,180,180]{3,2,1,0:T(8,128)(2,1)} %param.13) | copy-start | bytes 1749604
  128.1 32.2 %collective-permute-start.17 = (bf16[2,180,4,1]{1,3,2,0:T(2,128)(2,1)S(1)}, bf16[2,180,4,1]{1,3,2,0:T(2,128)(2,1)S(1)}, u32[]{:S(2)}, u32[]{:S(2)}) collective-permute-start(bf16[2,180,4,1]{1,3,2,0:T(2,128)(2,1)S(1)} %get-tuple-element.38), channel_id=1, source_target_pairs={{3,0},{0,1},{1,2},{2,3},{7,4},{4,5},{5,6},{6,7},{11,8},{8,9},{9,10... | collective-permute-start | bytes 8648 | tf_op jit(solution)/shard_map/ppermute | solution.py:10
  128.2 16.5 %collective-permute-start.16 = (bf16[2,180,1,16]{1,3,2,0:T(8,128)(2,1)S(1)}, bf16[2,180,1,16]{1,3,2,0:T(8,128)(2,1)S(1)}, u32[]{:S(2)}, u32[]{:S(2)}) collective-permute-start(bf16[2,180,1,16]{1,3,2,0:T(8,128)(2,1)S(1)} %pad_maximum_fusion.102), channel_id=1, source_target_pairs={{3,0},{0,1},{1,2},{2,3},{7,4},{4,5},{5,6},{6,7},{11,8},{8,9},{9,10... | collective-permute-start | bytes 34568 | tf_op jit(solution)/shard_map/ppermute | solution.py:10
  129.8 1.7 collective-permute-start.15
  160.4 4.0 %collective-permute-start.19 = (bf16[3,180,1,18]{1,3,2,0:T(8,128)(2,1)S(1)}, bf16[3,180,1,18]{1,3,2,0:T(8,128)(2,1)S(1)}, u32[]{:S(2)}, u32[]{:S(2)}) collective-permute-start(bf16[3,180,1,18]{1,3,2,0:T(8,128)(2,1)S(1)} %get-tuple-element.36), channel_id=1, source_target_pairs={{4,0},{8,4},{12,8},{0,12},{5,1},{9,5},{13,9},{1,13},{6,2},{10,6},{... | collective-permute-start | bytes 58328 | tf_op jit(solution)/shard_map/ppermute | solution.py:21
  161.4 5.8 %collective-permute-start.18 = (bf16[3,180,1,18]{1,3,2,0:T(8,128)(2,1)S(1)}, bf16[3,180,1,18]{1,3,2,0:T(8,128)(2,1)S(1)}, u32[]{:S(2)}, u32[]{:S(2)}) collective-permute-start(bf16[3,180,1,18]{1,3,2,0:T(8,128)(2,1)S(1)} %get-tuple-element.37), channel_id=1, source_target_pairs={{0,4},{4,8},{8,12},{12,0},{1,5},{5,9},{9,13},{13,1},{2,6},{6,10},{... | collective-permute-start | bytes 58328 | tf_op jit(solution)/shard_map/ppermute | solution.py:20
  170.2 33.1 %collective-permute-start.22 = (bf16[2,270,8,1]{1,2,3,0:T(8,128)(2,1)S(1)}, bf16[2,270,8,1]{1,2,3,0:T(8,128)(2,1)S(1)}, u32[]{:S(2)}, u32[]{:S(2)}) collective-permute-start(bf16[2,270,8,1]{1,2,3,0:T(8,128)(2,1)S(1)} %get-tuple-element.12), channel_id=1, source_target_pairs={{3,0},{0,1},{1,2},{2,3},{7,4},{4,5},{5,6},{6,7},{11,8},{8,9},{9,10... | collective-permute-start | bytes 25928 | tf_op jit(solution)/shard_map/ppermute | solution.py:10
  170.3 3.5 %collective-permute-start.20 = (bf16[4,270,8,1]{1,2,3,0:T(8,128)(2,1)S(1)}, bf16[4,270,8,1]{1,2,3,0:T(8,128)(2,1)S(1)}, u32[]{:S(2)}, u32[]{:S(2)}) collective-permute-start(bf16[4,270,8,1]{1,2,3,0:T(8,128)(2,1)S(1)} %pad_maximum_fusion.95), channel_id=1, source_target_pairs={{1,0},{2,1},{3,2},{0,3},{5,4},{6,5},{7,6},{4,7},{9,8},{10,9},{11,1... | collective-permute-start | bytes 51848 | tf_op jit(solution)/shard_map/ppermute | solution.py:10
  172.4 14.5 %collective-permute-start.21 = (bf16[2,270,1,32]{1,2,3,0:T(2,128)(2,1)S(1)}, bf16[2,270,1,32]{1,2,3,0:T(2,128)(2,1)S(1)}, u32[]{:S(2)}, u32[]{:S(2)}) collective-permute-start(bf16[2,270,1,32]{1,2,3,0:T(2,128)(2,1)S(1)} %pad_maximum_fusion.31), channel_id=1, source_target_pairs={{3,0},{0,1},{1,2},{2,3},{7,4},{4,5},{5,6},{6,7},{11,8},{8,9},{9,10... | collective-permute-start | bytes 103688 | tf_op jit(solution)/shard_map/ppermute | solution.py:10
  204.0 4.6 %collective-permute-start.24 = (bf16[3,270,1,34]{1,3,2,0:T(8,128)(2,1)S(1)}, bf16[3,270,1,34]{1,3,2,0:T(8,128)(2,1)S(1)}, u32[]{:S(2)}, u32[]{:S(2)}) collective-permute-start(bf16[3,270,1,34]{1,3,2,0:T(8,128)(2,1)S(1)} %get-tuple-element.7), channel_id=1, source_target_pairs={{4,0},{8,4},{12,8},{0,12},{5,1},{9,5},{13,9},{1,13},{6,2},{10,6},{... | collective-permute-start | bytes 165248 | tf_op jit(solution)/shard_map/ppermute | solution.py:21
  205.9 6.3 %collective-permute-start.23 = (bf16[3,270,1,34]{1,3,2,0:T(8,128)(2,1)S(1)}, bf16[3,270,1,34]{1,3,2,0:T(8,128)(2,1)S(1)}, u32[]{:S(2)}, u32[]{:S(2)}) collective-permute-start(bf16[3,270,1,34]{1,3,2,0:T(8,128)(2,1)S(1)} %get-tuple-element.8), channel_id=1, source_target_pairs={{0,4},{4,8},{8,12},{12,0},{1,5},{5,9},{9,13},{13,1},{2,6},{6,10},{... | collective-permute-start | bytes 165248 | tf_op jit(solution)/shard_map/ppermute | solution.py:20
  212.5 1.1 copy-start.4
  215.9 0.7 copy-start.7
Sparse Core Ops, SparseCore 0:
  60.0 17.1 reduce-scatter.6
where the time goes:
time: 225 us
  blocking collectives  132 us (59%)
  waiting for transfers between devices  32 us (14%)
  starting transfers between devices  21.5 us (10%)
  between operations  15.9 us (7%)
  matrix products  11.8 us (5%)
  local copies, waits for them, and re-layouts  7.52 us (3%)
  other arithmetic  3.83 us (2%)
    all_gather x5, blocking collectives, pad_strip(): lax.all_gather(following_sunrise_neighbour[2:], 'tile', axis=2, tiled=True)  66.1 us
    unnamed x4, blocking collectives  66 us
    ppermute x5, waiting for transfers between devices, padded_2(): before = lax.ppermute(last, axis, up)  13.5 us
    ppermute x15, starting transfers between devices, passed_along(): return lax.ppermute(block, axis, route)  11 us
    dot_general x43, matrix products, convolve(): jnp.einsum('oc,fcrn->forn', weight[row_tap, col_tap], window_patch, prefe...  10.8 us
    ppermute x5, waiting for transfers between devices, padded_2(): after = lax.ppermute(initial, axis, down)  9.37 us
    ppermute x5, starting transfers between devices, padded_2(): before = lax.ppermute(last, axis, up)  6.09 us
    ppermute x15, waiting for transfers between devices, passed_along(): return lax.ppermute(block, axis, route)  5.03 us
  transfers between devices with their start and end apart: 26, of which 16 were waited for; matrix products, arithmetic and copies ran while one was open for 2% of the time, Pallas kernels for 0%

commit v1 on v0

--- a/solution.py
+++ b/solution.py
@@ -2,6 +2,12 @@
 import jax.numpy as jnp
 from jax import lax
 from jax.sharding import PartitionSpec as P
+
+
+def joined_along(parts, dim):
+    parts = jnp.moveaxis(parts, 0, dim)
+    dims = parts.shape
+    return parts.reshape(*dims[:dim], dims[dim] * dims[dim + 1], *dims[dim + 2 :])
 
 
 def passed_along(block, axis, distance):
@@ -54,7 +60,20 @@
         ]
     )
     following_sunrise_neighbour = passed_along(east_cols, "face", -1)
-    polar_cols = lax.all_gather(following_sunrise_neighbour[2:], "tile", axis=2, tiled=True)
+    x = following_sunrise_neighbour[2:]
+    size_2 = lax.axis_size("tile")
+    pairs = [(i_2, (i_2 + 1) % size_2) for i_2 in range(size_2)]
+    back = [(b, a) for a, b in pairs]
+    lower, upper = ([], [])
+    for turn in range(size_2 - 1):
+        if turn % 2 == 0:
+            lower.append(lax.ppermute(lower[-1] if lower else x, "tile", pairs))
+        else:
+            upper.append(lax.ppermute(upper[-1] if upper else x, "tile", back))
+    blocks = jnp.stack([*lower[::-1], x, *upper])
+    shift = lax.axis_index("tile") - len(lower)
+    blocks = blocks[(jnp.arange(size_2) - shift) % size_2]
+    polar_cols = joined_along(blocks, 2)
     owner_mask = jnp.stack([tile_pos == 0, tile_pos == tile_count - 1]).reshape(2, 1, 1, 1)
     masked_rows = jnp.where(owner_mask, polar_prev, jnp.zeros_like(polar_prev)).astype(jnp.float32)
     pieces = lax.psum_scatter(

time: 225 us -> 204 us (0.907)
  blocking collectives: 132 us -> 77.6 us
  starting transfers between devices: 21.5 us -> 49.8 us
  local copies, waits for them, and re-layouts: 7.52 us -> 10.2 us
  waiting for transfers between devices: 32 us -> 34.5 us
    all_gather x5 -> x0, blocking collectives: 66.1 us -> none  [pad_strip(): lax.all_gather(following_sunrise_neighbour[2:], 'tile', axis=2, tiled=True)]
    ppermute x0 -> x15, starting transfers between devices: none -> 20.4 us  [the longest x5 17.8 us: pad_strip(): upper.append(lax.ppermute(upper[-1] if upper else x, 'tile', back))]
    ppermute x5, starting transfers between devices: 4.46 us -> 19.3 us  [padded_2(): after = lax.ppermute(initial, axis, down)]
    unnamed x4, blocking collectives: 66 us -> 77.6 us
    unnamed x2, waiting for transfers between devices: 4.16 us -> 15.2 us
    ppermute x0 -> x15, waiting for transfers between devices: none -> 9.98 us  [the longest x10 9.97 us: pad_strip(): lower.append(lax.ppermute(lower[-1] if lower else x, 'tile', pairs))]
    ppermute x5, waiting for transfers between devices: 9.37 us -> 0.01 us  [padded_2(): after = lax.ppermute(initial, axis, down)]
    ppermute x5, starting transfers between devices: 6.09 us -> 0.29 us  [padded_2(): before = lax.ppermute(last, axis, up)]
  transfers between devices with their start and end apart: 26 -> 41, of which waited for: 16 -> 14; matrix products, arithmetic and copies ran while one was open for 2% -> 4% of each run, Pallas kernels for 0% -> 0%
where the time goes in v1:
time: 204 us
  blocking collectives  77.6 us (38%)
  starting transfers between devices  49.8 us (24%)
  waiting for transfers between devices  34.5 us (17%)
  between operations  16.2 us (8%)
  matrix products  12.1 us (6%)
  local copies, waits for them, and re-layouts  10.2 us (5%)
  other arithmetic  3.36 us (2%)
    unnamed x4, blocking collectives  77.6 us
    ppermute x5, starting transfers between devices, padded_2(): after = lax.ppermute(initial, axis, down)  19.3 us
    ppermute x5, starting transfers between devices, pad_strip(): upper.append(lax.ppermute(upper[-1] if upper else x, 'tile', back))  17.8 us
    unnamed x2, waiting for transfers between devices  15.2 us
    dot_general x43, matrix products, convolve(): jnp.einsum('oc,fcrn->forn', weight[row_tap, col_tap], window_patch, prefe...  11.1 us
    ppermute x10, waiting for transfers between devices, pad_strip(): lower.append(lax.ppermute(lower[-1] if lower else x, 'tile', pairs))  9.97 us
    ppermute x15, starting transfers between devices, passed_along(): return lax.ppermute(block, axis, route)  9.7 us
    ppermute x5, waiting for transfers between devices, padded_2(): before = lax.ppermute(last, axis, up)  8.76 us
  transfers between devices with their start and end apart: 41, of which 14 were waited for; matrix products, arithmetic and copies ran while one was open for 4% of the time, Pallas kernels for 0%

profile of v1, /device:TPU:0, one launch (start us, length us, event | category | flops | bytes accessed | tf_op | source)
XLA Modules:
  0.0 203.8 jit_solution(657361132397326893)
XLA Ops:
  6.6 1.1 copy.374
  7.7 0.5 collective-permute-start.4
  8.8 2.0 collective-permute-start
  10.8 0.7 collective-permute-start.5
  12.2 2.4 %collective-permute-start.1 = (bf16[2,16,8,1]{1,2,3,0:T(8,128)(2,1)S(1)}, bf16[2,16,8,1]{1,2,3,0:T(8,128)(2,1)S(1)}, u32[]{:S(2)}, u32[]{:S(2)}) collective-permute-start(bf16[2,16,8,1]{1,2,3,0:T(8,128)(2,1)S(1)} %get-tuple-element.100), channel_id=1, source_target_pairs={{0,4},{4,8},{8,12},{12,0},{1,5},{5,9},{9,13},{13,1},{2,6},{6,10},{... | collective-permute-start | bytes 1544 | tf_op jit(solution)/shard_map/ppermute | solution.py:70
  14.5 0.6 dynamic-slice
  16.4 2.1 %collective-permute-start.3 = (bf16[2,16,8,1]{1,2,3,0:T(8,128)(2,1)S(1)}, bf16[2,16,8,1]{1,2,3,0:T(8,128)(2,1)S(1)}, u32[]{:S(2)}, u32[]{:S(2)}) collective-permute-start(bf16[2,16,8,1]{1,2,3,0:T(8,128)(2,1)S(1)} %get-tuple-element.100), channel_id=1, source_target_pairs={{4,0},{8,4},{12,8},{0,12},{5,1},{9,5},{13,9},{1,13},{6,2},{10,6},{... | collective-permute-start | bytes 1544 | tf_op jit(solution)/shard_map/ppermute | solution.py:72
  18.7 19.2 %all-reduce = bf16[2,16,1,32]{1,0,2,3:T(2,128)(2,1)S(1)} all-reduce(bf16[2,16,1,32]{1,0,2,3:T(2,128)(2,1)S(1)} %copy.161), channel_id=2, replica_groups=mesh['member'=2,'tile'=4,'face'=4] {'tile'}, use_global_device_ids=true, to_apply=%region_0.1.clone | all-reduce | flops 1024 | bytes 4096
  38.5 3.8 %collective-permute-start.7 = (bf16[3,16,1,34]{3,1,2,0:T(8,128)(2,1)S(1)}, bf16[3,16,1,34]{3,1,2,0:T(8,128)(2,1)S(1)}, u32[]{:S(2)}, u32[]{:S(2)}) collective-permute-start(bf16[3,16,1,34]{3,1,2,0:T(8,128)(2,1)S(1)} %get-tuple-element.11), channel_id=1, source_target_pairs={{4,0},{8,4},{12,8},{0,12},{5,1},{9,5},{13,9},{1,13},{6,2},{10,6},{... | collective-permute-start | bytes 9800 | tf_op jit(solution)/shard_map/ppermute | solution.py:27
  42.3 0.6 gather_fusion
  43.1 0.9 collective-permute-done.6
  47.5 0.5 collective-permute-start.12
  48.1 1.4 collective-permute-start.13
  49.5 3.8 %collective-permute-start.11 = (bf16[2,90,8,1]{1,3,2,0:T(2,128)(2,1)S(1)}, bf16[2,90,8,1]{1,3,2,0:T(2,128)(2,1)S(1)}, u32[]{:S(2)}, u32[]{:S(2)}) collective-permute-start(bf16[2,90,8,1]{1,3,2,0:T(2,128)(2,1)S(1)} %get-tuple-element.83), channel_id=1, source_target_pairs={{4,0},{8,4},{12,8},{0,12},{5,1},{9,5},{13,9},{1,13},{6,2},{10,6},{... | collective-permute-start | bytes 8648 | tf_op jit(solution)/shard_map/ppermute | solution.py:72
  53.6 1.4 collective-permute-done.9
  55.2 0.7 reshape.208
  55.9 4.5 %collective-permute-done.10 = bf16[2,90,8,1]{1,3,2,0:T(2,128)(2,1)S(1)} collective-permute-done((bf16[2,90,8,1]{1,3,2,0:T(2,128)(2,1)S(1)}, bf16[2,90,8,1]{1,3,2,0:T(2,128)(2,1)S(1)}, u32[]{:S(2)}, u32[]{:S(2)}) %collective-permute-start.10) | collective-permute-done | bytes 2912 | tf_op jit(solution)/shard_map/ppermute | solution.py:70
  60.4 0.6 gather_fusion.1
  61.0 15.1 %reduce-scatter.7.cloned.1.call-done = bf16[8,180]{1,0:T(8,128)(2,1)} async-done(((bf16[32,180]{1,0:T(8,128)(2,1)}), bf16[8,180]{1,0:T(8,128)(2,1)}) %reduce-scatter.7.cloned.1.call-update) | async-done | bytes 2896
  76.1 0.8 reshape.209
  77.1 3.8 %collective-permute-start.15 = (bf16[3,90,1,34]{1,3,2,0:T(8,128)(2,1)S(1)}, bf16[3,90,1,34]{1,3,2,0:T(8,128)(2,1)S(1)}, u32[]{:S(2)}, u32[]{:S(2)}) collective-permute-start(bf16[3,90,1,34]{1,3,2,0:T(8,128)(2,1)S(1)} %get-tuple-element.15), channel_id=1, source_target_pairs={{4,0},{8,4},{12,8},{0,12},{5,1},{9,5},{13,9},{1,13},{6,2},{10,6},{... | collective-permute-start | bytes 55088 | tf_op jit(solution)/shard_map/ppermute | solution.py:27
  80.9 1.9 collective-permute-done.14
  85.6 0.5 collective-permute-start.20
  86.2 1.1 collective-permute-start.21
  87.6 3.9 %collective-permute-start.19 = (bf16[2,90,4,2]{1,3,2,0:T(2,128)(2,1)S(1)}, bf16[2,90,4,2]{1,3,2,0:T(2,128)(2,1)S(1)}, u32[]{:S(2)}, u32[]{:S(2)}) collective-permute-start(bf16[2,90,4,2]{1,3,2,0:T(2,128)(2,1)S(1)} %get-tuple-element.95), channel_id=1, source_target_pairs={{4,0},{8,4},{12,8},{0,12},{5,1},{9,5},{13,9},{1,13},{6,2},{10,6},{... | collective-permute-start | bytes 8648 | tf_op jit(solution)/shard_map/ppermute | solution.py:72
  91.4 1.3 collective-permute-done.17
  92.9 19.2 %all-reduce.1 = bf16[2,90,2,16]{1,2,3,0:T(2,128)(2,1)S(1)} all-reduce(bf16[2,90,2,16]{1,2,3,0:T(2,128)(2,1)S(1)} %copy.172), channel_id=4, replica_groups=mesh['member'=2,'tile'=4,'face'=4] {'tile'}, use_global_device_ids=true, to_apply=%region_3.4.clone | all-reduce | flops 5760 | bytes 23040
  112.2 0.6 gather_fusion.2
  113.0 3.9 %collective-permute-start.23 = (bf16[3,90,2,20]{1,3,2,0:T(8,128)(2,1)S(1)}, bf16[3,90,2,20]{1,3,2,0:T(8,128)(2,1)S(1)}, u32[]{:S(2)}, u32[]{:S(2)}) collective-permute-start(bf16[3,90,2,20]{1,3,2,0:T(8,128)(2,1)S(1)} %get-tuple-element.43), channel_id=1, source_target_pairs={{4,0},{8,4},{12,8},{0,12},{5,1},{9,5},{13,9},{1,13},{6,2},{10,6},{... | collective-permute-start | bytes 64808 | tf_op jit(solution)/shard_map/ppermute | solution.py:27
  116.9 1.8 collective-permute-done.22
  121.3 0.8 collective-permute-start.29
  122.3 3.9 %collective-permute-start.27 = (bf16[2,180,4,1]{1,3,2,0:T(2,128)(2,1)S(1)}, bf16[2,180,4,1]{1,3,2,0:T(2,128)(2,1)S(1)}, u32[]{:S(2)}, u32[]{:S(2)}) collective-permute-start(bf16[2,180,4,1]{1,3,2,0:T(2,128)(2,1)S(1)} %get-tuple-element.73), channel_id=1, source_target_pairs={{4,0},{8,4},{12,8},{0,12},{5,1},{9,5},{13,9},{1,13},{6,2},{10,6},{... | collective-permute-start | bytes 8648 | tf_op jit(solution)/shard_map/ppermute | solution.py:72
  126.5 1.4 collective-permute-done.25
  128.0 19.3 %all-reduce.2 = bf16[2,180,1,16]{1,3,2,0:T(8,128)(2,1)S(1)} all-reduce(bf16[2,180,1,16]{1,3,2,0:T(8,128)(2,1)S(1)} %broadcast_select_fusion.1), channel_id=5, replica_groups=mesh['member'=2,'tile'=4,'face'=4] {'tile'}, use_global_device_ids=true, to_apply=%region_4.5.clone | all-reduce | flops 5760 | bytes 23040
  147.3 0.6 gather_fusion.3
  148.1 4.0 %collective-permute-start.31 = (bf16[3,180,1,18]{1,3,2,0:T(8,128)(2,1)S(1)}, bf16[3,180,1,18]{1,3,2,0:T(8,128)(2,1)S(1)}, u32[]{:S(2)}, u32[]{:S(2)}) collective-permute-start(bf16[3,180,1,18]{1,3,2,0:T(8,128)(2,1)S(1)} %get-tuple-element.25), channel_id=1, source_target_pairs={{4,0},{8,4},{12,8},{0,12},{5,1},{9,5},{13,9},{1,13},{6,2},{10,6},{... | collective-permute-start | bytes 58328 | tf_op jit(solution)/shard_map/ppermute | solution.py:27
  152.1 1.7 collective-permute-done.30
  156.8 0.5 collective-permute-start.37
  157.4 0.8 collective-permute-start.36
  158.6 4.1 %collective-permute-start.35 = (bf16[2,270,8,1]{1,3,2,0:T(2,128)(2,1)S(1)}, bf16[2,270,8,1]{1,3,2,0:T(2,128)(2,1)S(1)}, u32[]{:S(2)}, u32[]{:S(2)}) collective-permute-start(bf16[2,270,8,1]{1,3,2,0:T(2,128)(2,1)S(1)} %get-tuple-element.49), channel_id=1, source_target_pairs={{4,0},{8,4},{12,8},{0,12},{5,1},{9,5},{13,9},{1,13},{6,2},{10,6},{... | collective-permute-start | bytes 25928 | tf_op jit(solution)/shard_map/ppermute | solution.py:72
  163.1 1.3 collective-permute-done.33
  164.6 19.9 %all-reduce.3 = bf16[2,270,1,32]{1,3,2,0:T(8,128)(2,1)S(1)} all-reduce(bf16[2,270,1,32]{1,3,2,0:T(8,128)(2,1)S(1)} %broadcast_select_fusion), channel_id=6, replica_groups=mesh['member'=2,'tile'=4,'face'=4] {'tile'}, use_global_device_ids=true, to_apply=%region_5.6.clone | all-reduce | flops 17280 | bytes 69120
  184.6 0.6 gather_fusion.4
  185.4 3.8 %collective-permute-start.39 = (bf16[3,270,1,34]{1,3,2,0:T(8,128)(2,1)S(1)}, bf16[3,270,1,34]{1,3,2,0:T(8,128)(2,1)S(1)}, u32[]{:S(2)}, u32[]{:S(2)}) collective-permute-start(bf16[3,270,1,34]{1,3,2,0:T(8,128)(2,1)S(1)} %get-tuple-element.7), channel_id=1, source_target_pairs={{4,0},{8,4},{12,8},{0,12},{5,1},{9,5},{13,9},{1,13},{6,2},{10,6},{... | collective-permute-start | bytes 165248 | tf_op jit(solution)/shard_map/ppermute | solution.py:27
  189.2 2.5 %collective-permute-done.38 = bf16[3,270,1,34]{1,3,2,0:T(8,128)(2,1)S(1)} collective-permute-done((bf16[3,270,1,34]{1,3,2,0:T(8,128)(2,1)S(1)}, bf16[3,270,1,34]{1,3,2,0:T(8,128)(2,1)S(1)}, u32[]{:S(2)}, u32[]{:S(2)}) %collective-permute-start.38) | collective-permute-done | bytes 55112 | tf_op jit(solution)/shard_map/ppermute | solution.py:26
  192.0 0.7 pad_maximum_fusion
  195.6 0.6 fusion.11
  196.2 0.8 copy.178
  (272 shorter events, 19.6 us)
Async XLA Ops:
  6.5 78.1 %copy-start = (bf16[90,90]{1,0:T(8,128)(2,1)S(1)}, bf16[90,90]{1,0:T(8,128)(2,1)}, u32[]{:S(2)}) copy-start(bf16[90,90]{1,0:T(8,128)(2,1)} %param.11) | copy-start | bytes 48604
  6.5 8.0 %copy-start.8 = (u32[32]{0:T(128)S(1)}, u32[32]{0:T(128)}, u32[]{:S(2)}) copy-start(u32[32]{0:T(128)} %constant.70) | copy-start | bytes 388
  6.5 5.0 %copy-start.1 = (f32[3,1,16,8,32]{4,3,2,1,0:T(8,128)S(1)}, f32[3,1,16,8,32]{4,3,2,1,0:T(8,128)}, u32[]{:S(2)}) copy-start(f32[3,1,16,8,32]{4,3,2,1,0:T(8,128)} %param.8) | copy-start | bytes 147460
  6.5 5.0 %copy-start.6 = (bf16[3,3,90,16]{2,3,1,0:T(8,128)(2,1)S(1)}, bf16[3,3,90,16]{2,3,1,0:T(8,128)(2,1)}, u32[]{:S(2)}) copy-start(bf16[3,3,90,16]{2,3,1,0:T(8,128)(2,1)} %param.9) | copy-start | bytes 77764
  6.5 69.6 %reduce-scatter.7.cloned.1.call-start = ((), (), s32[]{:S(2)}) async-start(), calls=%async_computation.1 | async-start | bytes 20480
  7.7 10.9 %collective-permute-start.4 = (bf16[2,16,1,32]{3,1,2,0:T(8,128)(2,1)S(1)}, bf16[2,16,1,32]{3,1,2,0:T(8,128)(2,1)S(1)}, u32[]{:S(2)}, u32[]{:S(2)}) collective-permute-start(bf16[2,16,1,32]{3,1,2,0:T(8,128)(2,1)S(1)} %pad_maximum_fusion.118), channel_id=1, source_target_pairs={{3,0},{0,1},{1,2},{2,3},{7,4},{4,5},{5,6},{6,7},{11,8},{8,9},{9,10... | collective-permute-start | bytes 6152 | tf_op jit(solution)/shard_map/ppermute | solution.py:16
  8.8 3.4 %collective-permute-start = (bf16[4,16,8,1]{1,2,3,0:T(8,128)(2,1)S(1)}, bf16[4,16,8,1]{1,2,3,0:T(8,128)(2,1)S(1)}, u32[]{:S(2)}, u32[]{:S(2)}) collective-permute-start(bf16[4,16,8,1]{1,2,3,0:T(8,128)(2,1)S(1)} %pad_maximum_fusion.117), channel_id=1, source_target_pairs={{1,0},{2,1},{3,2},{0,3},{5,4},{6,5},{7,6},{4,7},{9,8},{10,9},{11,1... | collective-permute-start | bytes 3080 | tf_op jit(solution)/shard_map/ppermute | solution.py:16
  10.8 27.6 %collective-permute-start.5 = (bf16[2,16,8,1]{3,1,2,0:T(8,128)(2,1)S(1)}, bf16[2,16,8,1]{3,1,2,0:T(8,128)(2,1)S(1)}, u32[]{:S(2)}, u32[]{:S(2)}) collective-permute-start(bf16[2,16,8,1]{3,1,2,0:T(8,128)(2,1)S(1)} %get-tuple-element.33), channel_id=1, source_target_pairs={{3,0},{0,1},{1,2},{2,3},{7,4},{4,5},{5,6},{6,7},{11,8},{8,9},{9,10... | collective-permute-start | bytes 1544 | tf_op jit(solution)/shard_map/ppermute | solution.py:16
  12.2 6.4 %collective-permute-start.1 = (bf16[2,16,8,1]{1,2,3,0:T(8,128)(2,1)S(1)}, bf16[2,16,8,1]{1,2,3,0:T(8,128)(2,1)S(1)}, u32[]{:S(2)}, u32[]{:S(2)}) collective-permute-start(bf16[2,16,8,1]{1,2,3,0:T(8,128)(2,1)S(1)} %get-tuple-element.100), channel_id=1, source_target_pairs={{0,4},{4,8},{8,12},{12,0},{1,5},{5,9},{9,13},{13,1},{2,6},{6,10},{... | collective-permute-start | bytes 1544 | tf_op jit(solution)/shard_map/ppermute | solution.py:70
  16.4 25.9 %collective-permute-start.3 = (bf16[2,16,8,1]{1,2,3,0:T(8,128)(2,1)S(1)}, bf16[2,16,8,1]{1,2,3,0:T(8,128)(2,1)S(1)}, u32[]{:S(2)}, u32[]{:S(2)}) collective-permute-start(bf16[2,16,8,1]{1,2,3,0:T(8,128)(2,1)S(1)} %get-tuple-element.100), channel_id=1, source_target_pairs={{4,0},{8,4},{12,8},{0,12},{5,1},{9,5},{13,9},{1,13},{6,2},{10,6},{... | collective-permute-start | bytes 1544 | tf_op jit(solution)/shard_map/ppermute | solution.py:72
  18.5 23.8 %collective-permute-start.2 = (bf16[2,16,8,1]{1,2,3,0:T(8,128)(2,1)S(1)}, bf16[2,16,8,1]{1,2,3,0:T(8,128)(2,1)S(1)}, u32[]{:S(2)}, u32[]{:S(2)}) collective-permute-start(bf16[2,16,8,1]{1,2,3,0:T(8,128)(2,1)S(1)} %collective-permute-done.1), channel_id=1, source_target_pairs={{0,4},{4,8},{8,12},{12,0},{1,5},{5,9},{9,13},{13,1},{2,6},{6,10},{... | collective-permute-start | bytes 1544 | tf_op jit(solution)/shard_map/ppermute | solution.py:70
  38.4 5.5 %collective-permute-start.6 = (bf16[3,16,1,34]{3,1,2,0:T(8,128)(2,1)S(1)}, bf16[3,16,1,34]{3,1,2,0:T(8,128)(2,1)S(1)}, u32[]{:S(2)}, u32[]{:S(2)}) collective-permute-start(bf16[3,16,1,34]{3,1,2,0:T(8,128)(2,1)S(1)} %get-tuple-element.12), channel_id=1, source_target_pairs={{0,4},{4,8},{8,12},{12,0},{1,5},{5,9},{9,13},{13,1},{2,6},{6,10},{... | collective-permute-start | bytes 9800 | tf_op jit(solution)/shard_map/ppermute | solution.py:26
  38.5 5.6 %collective-permute-start.7 = (bf16[3,16,1,34]{3,1,2,0:T(8,128)(2,1)S(1)}, bf16[3,16,1,34]{3,1,2,0:T(8,128)(2,1)S(1)}, u32[]{:S(2)}, u32[]{:S(2)}) collective-permute-start(bf16[3,16,1,34]{3,1,2,0:T(8,128)(2,1)S(1)} %get-tuple-element.11), channel_id=1, source_target_pairs={{4,0},{8,4},{12,8},{0,12},{5,1},{9,5},{13,9},{1,13},{6,2},{10,6},{... | collective-permute-start | bytes 9800 | tf_op jit(solution)/shard_map/ppermute | solution.py:27
  46.9 6.4 %copy-start.4 = (bf16[3,3,90,90]{3,2,1,0:T(8,128)(2,1)S(1)}, bf16[3,3,90,90]{3,2,1,0:T(8,128)(2,1)}, u32[]{:S(2)}) copy-start(bf16[3,3,90,90]{3,2,1,0:T(8,128)(2,1)} %param.10) | copy-start | bytes 437404
  47.4 2.0 collective-permute-start.8
  47.5 7.5 %collective-permute-start.12 = (bf16[2,90,1,32]{1,3,2,0:T(8,128)(2,1)S(1)}, bf16[2,90,1,32]{1,3,2,0:T(8,128)(2,1)S(1)}, u32[]{:S(2)}, u32[]{:S(2)}) collective-permute-start(bf16[2,90,1,32]{1,3,2,0:T(8,128)(2,1)S(1)} %pad_maximum_fusion.96), channel_id=1, source_target_pairs={{3,0},{0,1},{1,2},{2,3},{7,4},{4,5},{5,6},{6,7},{11,8},{8,9},{9,10... | collective-permute-start | bytes 34568 | tf_op jit(solution)/shard_map/ppermute | solution.py:16
  48.1 28.9 %collective-permute-start.13 = (bf16[2,90,8,1]{1,3,2,0:T(2,128)(2,1)S(1)}, bf16[2,90,8,1]{1,3,2,0:T(2,128)(2,1)S(1)}, u32[]{:S(2)}, u32[]{:S(2)}) collective-permute-start(bf16[2,90,8,1]{1,3,2,0:T(2,128)(2,1)S(1)} %get-tuple-element.17), channel_id=1, source_target_pairs={{3,0},{0,1},{1,2},{2,3},{7,4},{4,5},{5,6},{6,7},{11,8},{8,9},{9,10... | collective-permute-start | bytes 8648 | tf_op jit(solution)/shard_map/ppermute | solution.py:16
  49.5 5.5 %collective-permute-start.9 = (bf16[2,90,8,1]{1,3,2,0:T(2,128)(2,1)S(1)}, bf16[2,90,8,1]{1,3,2,0:T(2,128)(2,1)S(1)}, u32[]{:S(2)}, u32[]{:S(2)}) collective-permute-start(bf16[2,90,8,1]{1,3,2,0:T(2,128)(2,1)S(1)} %get-tuple-element.83), channel_id=1, source_target_pairs={{0,4},{4,8},{8,12},{12,0},{1,5},{5,9},{9,13},{13,1},{2,6},{6,10},{... | collective-permute-start | bytes 8648 | tf_op jit(solution)/shard_map/ppermute | solution.py:70
  49.5 5.4 %collective-permute-start.11 = (bf16[2,90,8,1]{1,3,2,0:T(2,128)(2,1)S(1)}, bf16[2,90,8,1]{1,3,2,0:T(2,128)(2,1)S(1)}, u32[]{:S(2)}, u32[]{:S(2)}) collective-permute-start(bf16[2,90,8,1]{1,3,2,0:T(2,128)(2,1)S(1)} %get-tuple-element.83), channel_id=1, source_target_pairs={{4,0},{8,4},{12,8},{0,12},{5,1},{9,5},{13,9},{1,13},{6,2},{10,6},{... | collective-permute-start | bytes 8648 | tf_op jit(solution)/shard_map/ppermute | solution.py:72
  55.0 5.4 %collective-permute-start.10 = (bf16[2,90,8,1]{1,3,2,0:T(2,128)(2,1)S(1)}, bf16[2,90,8,1]{1,3,2,0:T(2,128)(2,1)S(1)}, u32[]{:S(2)}, u32[]{:S(2)}) collective-permute-start(bf16[2,90,8,1]{1,3,2,0:T(2,128)(2,1)S(1)} %collective-permute-done.9), channel_id=1, source_target_pairs={{0,4},{4,8},{8,12},{12,0},{1,5},{5,9},{9,13},{13,1},{2,6},{6,10},{... | collective-permute-start | bytes 8648 | tf_op jit(solution)/shard_map/ppermute | solution.py:70
  77.0 5.7 %collective-permute-start.14 = (bf16[3,90,1,34]{1,3,2,0:T(8,128)(2,1)S(1)}, bf16[3,90,1,34]{1,3,2,0:T(8,128)(2,1)S(1)}, u32[]{:S(2)}, u32[]{:S(2)}) collective-permute-start(bf16[3,90,1,34]{1,3,2,0:T(8,128)(2,1)S(1)} %get-tuple-element.16), channel_id=1, source_target_pairs={{0,4},{4,8},{8,12},{12,0},{1,5},{5,9},{9,13},{13,1},{2,6},{6,10},{... | collective-permute-start | bytes 55088 | tf_op jit(solution)/shard_map/ppermute | solution.py:26
  77.1 5.7 %collective-permute-start.15 = (bf16[3,90,1,34]{1,3,2,0:T(8,128)(2,1)S(1)}, bf16[3,90,1,34]{1,3,2,0:T(8,128)(2,1)S(1)}, u32[]{:S(2)}, u32[]{:S(2)}) collective-permute-start(bf16[3,90,1,34]{1,3,2,0:T(8,128)(2,1)S(1)} %get-tuple-element.15), channel_id=1, source_target_pairs={{4,0},{8,4},{12,8},{0,12},{5,1},{9,5},{13,9},{1,13},{6,2},{10,6},{... | collective-permute-start | bytes 55088 | tf_op jit(solution)/shard_map/ppermute | solution.py:27
  85.5 1.7 collective-permute-start.16
  85.6 7.1 %collective-permute-start.20 = (bf16[2,90,2,16]{1,3,2,0:T(8,128)(2,1)S(1)}, bf16[2,90,2,16]{1,3,2,0:T(8,128)(2,1)S(1)}, u32[]{:S(2)}, u32[]{:S(2)}) collective-permute-start(bf16[2,90,2,16]{1,3,2,0:T(8,128)(2,1)S(1)} %pad_maximum_fusion.98), channel_id=1, source_target_pairs={{3,0},{0,1},{1,2},{2,3},{7,4},{4,5},{5,6},{6,7},{11,8},{8,9},{9,10... | collective-permute-start | bytes 34568 | tf_op jit(solution)/shard_map/ppermute | solution.py:16
  86.2 26.7 %collective-permute-start.21 = (bf16[2,90,4,2]{1,3,2,0:T(2,128)(2,1)S(1)}, bf16[2,90,4,2]{1,3,2,0:T(2,128)(2,1)S(1)}, u32[]{:S(2)}, u32[]{:S(2)}) collective-permute-start(bf16[2,90,4,2]{1,3,2,0:T(2,128)(2,1)S(1)} %get-tuple-element.53), channel_id=1, source_target_pairs={{3,0},{0,1},{1,2},{2,3},{7,4},{4,5},{5,6},{6,7},{11,8},{8,9},{9,10... | collective-permute-start | bytes 8648 | tf_op jit(solution)/shard_map/ppermute | solution.py:16
  87.3 5.5 %collective-permute-start.17 = (bf16[2,90,4,2]{1,3,2,0:T(2,128)(2,1)S(1)}, bf16[2,90,4,2]{1,3,2,0:T(2,128)(2,1)S(1)}, u32[]{:S(2)}, u32[]{:S(2)}) collective-permute-start(bf16[2,90,4,2]{1,3,2,0:T(2,128)(2,1)S(1)} %get-tuple-element.95), channel_id=1, source_target_pairs={{0,4},{4,8},{8,12},{12,0},{1,5},{5,9},{9,13},{13,1},{2,6},{6,10},{... | collective-permute-start | bytes 8648 | tf_op jit(solution)/shard_map/ppermute | solution.py:70
  87.6 24.5 %collective-permute-start.19 = (bf16[2,90,4,2]{1,3,2,0:T(2,128)(2,1)S(1)}, bf16[2,90,4,2]{1,3,2,0:T(2,128)(2,1)S(1)}, u32[]{:S(2)}, u32[]{:S(2)}) collective-permute-start(bf16[2,90,4,2]{1,3,2,0:T(2,128)(2,1)S(1)} %get-tuple-element.95), channel_id=1, source_target_pairs={{4,0},{8,4},{12,8},{0,12},{5,1},{9,5},{13,9},{1,13},{6,2},{10,6},{... | collective-permute-start | bytes 8648 | tf_op jit(solution)/shard_map/ppermute | solution.py:72
  92.8 19.3 %collective-permute-start.18 = (bf16[2,90,4,2]{1,3,2,0:T(2,128)(2,1)S(1)}, bf16[2,90,4,2]{1,3,2,0:T(2,128)(2,1)S(1)}, u32[]{:S(2)}, u32[]{:S(2)}) collective-permute-start(bf16[2,90,4,2]{1,3,2,0:T(2,128)(2,1)S(1)} %collective-permute-done.17), channel_id=1, source_target_pairs={{0,4},{4,8},{8,12},{12,0},{1,5},{5,9},{9,13},{13,1},{2,6},{6,10},{... | collective-permute-start | bytes 8648 | tf_op jit(solution)/shard_map/ppermute | solution.py:70
  112.9 5.8 %collective-permute-start.22 = (bf16[3,90,2,20]{1,3,2,0:T(8,128)(2,1)S(1)}, bf16[3,90,2,20]{1,3,2,0:T(8,128)(2,1)S(1)}, u32[]{:S(2)}, u32[]{:S(2)}) collective-permute-start(bf16[3,90,2,20]{1,3,2,0:T(8,128)(2,1)S(1)} %get-tuple-element.44), channel_id=1, source_target_pairs={{0,4},{4,8},{8,12},{12,0},{1,5},{5,9},{9,13},{13,1},{2,6},{6,10},{... | collective-permute-start | bytes 64808 | tf_op jit(solution)/shard_map/ppermute | solution.py:26
  113.0 5.7 %collective-permute-start.23 = (bf16[3,90,2,20]{1,3,2,0:T(8,128)(2,1)S(1)}, bf16[3,90,2,20]{1,3,2,0:T(8,128)(2,1)S(1)}, u32[]{:S(2)}, u32[]{:S(2)}) collective-permute-start(bf16[3,90,2,20]{1,3,2,0:T(8,128)(2,1)S(1)} %get-tuple-element.43), channel_id=1, source_target_pairs={{4,0},{8,4},{12,8},{0,12},{5,1},{9,5},{13,9},{1,13},{6,2},{10,6},{... | collective-permute-start | bytes 64808 | tf_op jit(solution)/shard_map/ppermute | solution.py:27
  120.0 6.3 %copy-start.2 = (bf16[3,3,180,180]{3,2,1,0:T(8,128)(2,1)S(1)}, bf16[3,3,180,180]{3,2,1,0:T(8,128)(2,1)}, u32[]{:S(2)}) copy-start(bf16[3,3,180,180]{3,2,1,0:T(8,128)(2,1)} %param.13) | copy-start | bytes 1749604
  120.7 1.5 collective-permute-start.24
  120.8 7.0 %collective-permute-start.28 = (bf16[2,180,1,16]{1,3,2,0:T(8,128)(2,1)S(1)}, bf16[2,180,1,16]{1,3,2,0:T(8,128)(2,1)S(1)}, u32[]{:S(2)}, u32[]{:S(2)}) collective-permute-start(bf16[2,180,1,16]{1,3,2,0:T(8,128)(2,1)S(1)} %pad_maximum_fusion.100), channel_id=1, source_target_pairs={{3,0},{0,1},{1,2},{2,3},{7,4},{4,5},{5,6},{6,7},{11,8},{8,9},{9,10... | collective-permute-start | bytes 34568 | tf_op jit(solution)/shard_map/ppermute | solution.py:16
  121.3 26.6 %collective-permute-start.29 = (bf16[2,180,4,1]{1,3,2,0:T(2,128)(2,1)S(1)}, bf16[2,180,4,1]{1,3,2,0:T(2,128)(2,1)S(1)}, u32[]{:S(2)}, u32[]{:S(2)}) collective-permute-start(bf16[2,180,4,1]{1,3,2,0:T(2,128)(2,1)S(1)} %get-tuple-element.27), channel_id=1, source_target_pairs={{3,0},{0,1},{1,2},{2,3},{7,4},{4,5},{5,6},{6,7},{11,8},{8,9},{9,10... | collective-permute-start | bytes 8648 | tf_op jit(solution)/shard_map/ppermute | solution.py:16
  122.3 5.6 %collective-permute-start.25 = (bf16[2,180,4,1]{1,3,2,0:T(2,128)(2,1)S(1)}, bf16[2,180,4,1]{1,3,2,0:T(2,128)(2,1)S(1)}, u32[]{:S(2)}, u32[]{:S(2)}) collective-permute-start(bf16[2,180,4,1]{1,3,2,0:T(2,128)(2,1)S(1)} %get-tuple-element.73), channel_id=1, source_target_pairs={{0,4},{4,8},{8,12},{12,0},{1,5},{5,9},{9,13},{13,1},{2,6},{6,10},{... | collective-permute-start | bytes 8648 | tf_op jit(solution)/shard_map/ppermute | solution.py:70
  122.3 5.5 %collective-permute-start.27 = (bf16[2,180,4,1]{1,3,2,0:T(2,128)(2,1)S(1)}, bf16[2,180,4,1]{1,3,2,0:T(2,128)(2,1)S(1)}, u32[]{:S(2)}, u32[]{:S(2)}) collective-permute-start(bf16[2,180,4,1]{1,3,2,0:T(2,128)(2,1)S(1)} %get-tuple-element.73), channel_id=1, source_target_pairs={{4,0},{8,4},{12,8},{0,12},{5,1},{9,5},{13,9},{1,13},{6,2},{10,6},{... | collective-permute-start | bytes 8648 | tf_op jit(solution)/shard_map/ppermute | solution.py:72
  127.8 19.4 %collective-permute-start.26 = (bf16[2,180,4,1]{1,3,2,0:T(2,128)(2,1)S(1)}, bf16[2,180,4,1]{1,3,2,0:T(2,128)(2,1)S(1)}, u32[]{:S(2)}, u32[]{:S(2)}) collective-permute-start(bf16[2,180,4,1]{1,3,2,0:T(2,128)(2,1)S(1)} %collective-permute-done.25), channel_id=1, source_target_pairs={{0,4},{4,8},{8,12},{12,0},{1,5},{5,9},{9,13},{13,1},{2,6},{6,10},{... | collective-permute-start | bytes 8648 | tf_op jit(solution)/shard_map/ppermute | solution.py:70
  148.0 5.8 %collective-permute-start.30 = (bf16[3,180,1,18]{1,3,2,0:T(8,128)(2,1)S(1)}, bf16[3,180,1,18]{1,3,2,0:T(8,128)(2,1)S(1)}, u32[]{:S(2)}, u32[]{:S(2)}) collective-permute-start(bf16[3,180,1,18]{1,3,2,0:T(8,128)(2,1)S(1)} %get-tuple-element.26), channel_id=1, source_target_pairs={{0,4},{4,8},{8,12},{12,0},{1,5},{5,9},{9,13},{13,1},{2,6},{6,10},{... | collective-permute-start | bytes 58328 | tf_op jit(solution)/shard_map/ppermute | solution.py:26
  148.1 5.7 %collective-permute-start.31 = (bf16[3,180,1,18]{1,3,2,0:T(8,128)(2,1)S(1)}, bf16[3,180,1,18]{1,3,2,0:T(8,128)(2,1)S(1)}, u32[]{:S(2)}, u32[]{:S(2)}) collective-permute-start(bf16[3,180,1,18]{1,3,2,0:T(8,128)(2,1)S(1)} %get-tuple-element.25), channel_id=1, source_target_pairs={{4,0},{8,4},{12,8},{0,12},{5,1},{9,5},{13,9},{1,13},{6,2},{10,6},{... | collective-permute-start | bytes 58328 | tf_op jit(solution)/shard_map/ppermute | solution.py:27
  156.5 6.2 %copy-start.5 = (bf16[3,3,90,270]{2,3,1,0:T(8,128)(2,1)S(1)}, bf16[3,3,90,270]{2,3,1,0:T(8,128)(2,1)}, u32[]{:S(2)}) copy-start(bf16[3,3,90,270]{2,3,1,0:T(8,128)(2,1)} %param.14) | copy-start | bytes 1312204
  156.7 1.8 collective-permute-start.32
  156.8 28.3 %collective-permute-start.37 = (bf16[2,270,8,1]{1,3,2,0:T(2,128)(2,1)S(1)}, bf16[2,270,8,1]{1,3,2,0:T(2,128)(2,1)S(1)}, u32[]{:S(2)}, u32[]{:S(2)}) collective-permute-start(bf16[2,270,8,1]{1,3,2,0:T(2,128)(2,1)S(1)} %pad_maximum_fusion.94), channel_id=1, source_target_pairs={{3,0},{0,1},{1,2},{2,3},{7,4},{4,5},{5,6},{6,7},{11,8},{8,9},{9,10... | collective-permute-start | bytes 25928 | tf_op jit(solution)/shard_map/ppermute | solution.py:16
  157.4 7.1 %collective-permute-start.36 = (bf16[2,270,1,32]{1,3,2,0:T(8,128)(2,1)S(1)}, bf16[2,270,1,32]{1,3,2,0:T(8,128)(2,1)S(1)}, u32[]{:S(2)}, u32[]{:S(2)}) collective-permute-start(bf16[2,270,1,32]{1,3,2,0:T(8,128)(2,1)S(1)} %fusion.160), channel_id=1, source_target_pairs={{3,0},{0,1},{1,2},{2,3},{7,4},{4,5},{5,6},{6,7},{11,8},{8,9},{9,10... | collective-permute-start | bytes 103688 | tf_op jit(solution)/shard_map/ppermute | solution.py:16
  158.5 5.9 %collective-permute-start.33 = (bf16[2,270,8,1]{1,3,2,0:T(2,128)(2,1)S(1)}, bf16[2,270,8,1]{1,3,2,0:T(2,128)(2,1)S(1)}, u32[]{:S(2)}, u32[]{:S(2)}) collective-permute-start(bf16[2,270,8,1]{1,3,2,0:T(2,128)(2,1)S(1)} %get-tuple-element.49), channel_id=1, source_target_pairs={{0,4},{4,8},{8,12},{12,0},{1,5},{5,9},{9,13},{13,1},{2,6},{6,10},{... | collective-permute-start | bytes 25928 | tf_op jit(solution)/shard_map/ppermute | solution.py:70
  158.6 5.9 %collective-permute-start.35 = (bf16[2,270,8,1]{1,3,2,0:T(2,128)(2,1)S(1)}, bf16[2,270,8,1]{1,3,2,0:T(2,128)(2,1)S(1)}, u32[]{:S(2)}, u32[]{:S(2)}) collective-permute-start(bf16[2,270,8,1]{1,3,2,0:T(2,128)(2,1)S(1)} %get-tuple-element.49), channel_id=1, source_target_pairs={{4,0},{8,4},{12,8},{0,12},{5,1},{9,5},{13,9},{1,13},{6,2},{10,6},{... | collective-permute-start | bytes 25928 | tf_op jit(solution)/shard_map/ppermute | solution.py:72
  164.5 20.1 %collective-permute-start.34 = (bf16[2,270,8,1]{1,3,2,0:T(2,128)(2,1)S(1)}, bf16[2,270,8,1]{1,3,2,0:T(2,128)(2,1)S(1)}, u32[]{:S(2)}, u32[]{:S(2)}) collective-permute-start(bf16[2,270,8,1]{1,3,2,0:T(2,128)(2,1)S(1)} %collective-permute-done.33), channel_id=1, source_target_pairs={{0,4},{4,8},{8,12},{12,0},{1,5},{5,9},{9,13},{13,1},{2,6},{6,10},{... | collective-permute-start | bytes 25928 | tf_op jit(solution)/shard_map/ppermute | solution.py:70
  185.4 6.4 %collective-permute-start.38 = (bf16[3,270,1,34]{1,3,2,0:T(8,128)(2,1)S(1)}, bf16[3,270,1,34]{1,3,2,0:T(8,128)(2,1)S(1)}, u32[]{:S(2)}, u32[]{:S(2)}) collective-permute-start(bf16[3,270,1,34]{1,3,2,0:T(8,128)(2,1)S(1)} %get-tuple-element.8), channel_id=1, source_target_pairs={{0,4},{4,8},{8,12},{12,0},{1,5},{5,9},{9,13},{13,1},{2,6},{6,10},{... | collective-permute-start | bytes 165248 | tf_op jit(solution)/shard_map/ppermute | solution.py:26
  185.4 6.4 %collective-permute-start.39 = (bf16[3,270,1,34]{1,3,2,0:T(8,128)(2,1)S(1)}, bf16[3,270,1,34]{1,3,2,0:T(8,128)(2,1)S(1)}, u32[]{:S(2)}, u32[]{:S(2)}) collective-permute-start(bf16[3,270,1,34]{1,3,2,0:T(8,128)(2,1)S(1)} %get-tuple-element.7), channel_id=1, source_target_pairs={{4,0},{8,4},{12,8},{0,12},{5,1},{9,5},{13,9},{1,13},{6,2},{10,6},{... | collective-permute-start | bytes 165248 | tf_op jit(solution)/shard_map/ppermute | solution.py:27
  (2 other events, 3.4 us)
Sparse Core Ops, SparseCore 0:
  56.0 20.0 reduce-scatter.6
